TPU v7x, 32 devices: a whole 2x2x4 slice. The times are simulated.
32 devices in a mesh: gx: 8 (over z, y), gz: 4 (over x, core).
Axes of the slice: x: 2, y: 2, z: 4, core: 2. Of those that a mesh axis runs over, the one named last changes fastest.
Arguments:
- whitened: float32 [2, 64, 1024, 512], P(None, 'gz', 'gx'), may hold values from -6 to 6
- observed: float32 [2, 1024, 512], P(None, 'gx'), may hold values from -12 to 12
- lower_x: bfloat16 [1024, 1024], P('gx'), as said below
- lower_y: bfloat16 [512, 512], P('gx'), as said below
- lower_z: bfloat16 [64, 64], replicated, as said below
- coupling_kernel: float32 [2, 3, 3, 3], replicated, may hold values from -1.25 to 1.25
Outputs:
- gradient: float32 [2, 64, 1024, 512], P(None, 'gz', 'gx')
- misfit: float32 [2, 1024, 512], P(None, 'gx')
Inputs may be any that keep to these rules, and one draw needn't show every extreme that they name: `lower_x`: lower triangular: zero above the diagonal, diagonal entries between 0.5 and 1.5. `lower_y`: lower triangular: zero above the diagonal, diagonal entries between 0.5 and 1.5. `lower_z`: lower triangular: zero above the diagonal, diagonal entries between 0.5 and 1.5.
All inputs are finite; a program needn't handle non-finite values.
Results may differ from a plain program's by a relative error of at most 0.013.
The roundings to bfloat16 on the way count: a program that leaves them out, or rounds other values in their place, can miss the bound.
Values may be sent and summed in bfloat16 or wider, within the bound.
A program may use at most 128 MiB of HBM per device.

v0:
```python
import math
import jax
import jax.numpy as jnp
from jax import lax
from jax.sharding import PartitionSpec as P

NZ = 64


def padded_2(x, sides, width):
    for axis, dim in sides:
        peers, length = (lax.axis_size(axis), x.shape[dim])
        up = [(i, (i + 1) % peers) for i in range(peers - 1)]
        down = [(j, i) for i, j in up]
        last = lax.slice_in_dim(x, length - width, length, axis=dim)
        first = lax.slice_in_dim(x, 0, width, axis=dim)
        before = lax.ppermute(last, axis, up)
        after = lax.ppermute(first, axis, down)
        x = jnp.concatenate([before, x, after], axis=dim)
    return x


def depth_lines(values, local_step):
    turned = lax.all_to_all(values, "gz", split_axis=3, concat_axis=1, tiled=True)
    return lax.all_to_all(local_step(turned), "gz", split_axis=1, concat_axis=3, tiled=True)


def across_lines(values, local_step):
    turned = lax.all_to_all(values, "gx", split_axis=3, concat_axis=2, tiled=True)
    return lax.all_to_all(local_step(turned), "gx", split_axis=2, concat_axis=3, tiled=True)


def stencil_sum(padded, kernel, depth_rows, x_rows, y_rows, flipped):
    total = jnp.zeros(padded.shape[:-3] + (depth_rows, x_rows, y_rows), jnp.float32)
    for offset_z in range(3):
        for offset_x in range(3):
            for offset_y in range(3):
                start_z = 2 - offset_z if flipped else offset_z
                start_x = 2 - offset_x if flipped else offset_x
                start_y = 2 - offset_y if flipped else offset_y
                total = (
                    total
                    + kernel[offset_z, offset_x, offset_y]
                    * padded[
                        ...,
                        start_z : start_z + depth_rows,
                        start_x : start_x + x_rows,
                        start_y : start_y + y_rows,
                    ]
                )
    return total


def depth_weights(first_row, depth_rows):
    depth = (first_row + jnp.arange(depth_rows)).astype(jnp.float32)
    factor = 4.0 / math.sqrt(NZ)
    return (factor / (1.0 + depth / NZ) ** 2, factor / (1.0 + depth / NZ) ** 3)


def coupling_forward(rim, magnetic_f, kernel, shape):
    depth_rows, x_rows, y_rows = shape
    pre_scale = stencil_sum(rim, kernel[0], depth_rows, x_rows, y_rows, False)
    pre_shift = stencil_sum(rim, kernel[1], depth_rows, x_rows, y_rows, False)
    scale = jnp.tanh(pre_scale)
    growth = jnp.exp(scale)
    return (scale, growth, magnetic_f * growth + pre_shift)


def local(whitened, observed, lower_x, lower_y, lower_z, coupling_kernel):
    factor_x, factor_y = (
        lax.all_gather(lower_x, "gx", axis=0, tiled=True),
        lax.all_gather(lower_y, "gx", axis=0, tiled=True),
    )

    def apply_depth(values):
        return jnp.einsum(
            "zk,fkxy->fzxy", lower_z, values, preferred_element_type=jnp.float32
        ).astype(jnp.bfloat16)

    def apply_across(values):
        return jnp.einsum(
            "xk,fzky->fzxy", factor_x, values, preferred_element_type=jnp.float32
        ).astype(jnp.bfloat16)

    def depth_adjoint(values):
        return jnp.einsum(
            "kz,fkxy->fzxy", lower_z, values, preferred_element_type=jnp.float32
        ).astype(jnp.bfloat16)

    def across_adjoint(values):
        return jnp.einsum(
            "kx,fzky->fzxy", factor_x, values, preferred_element_type=jnp.float32
        ).astype(jnp.bfloat16)

    start = whitened.astype(jnp.bfloat16)
    first = jnp.einsum("fzxk,yk->fzxy", start, factor_y, preferred_element_type=jnp.float32).astype(
        jnp.bfloat16
    )
    model = across_lines(depth_lines(first, apply_depth), apply_across)
    density = model[0]
    magnetic_f = model[1].astype(jnp.float32)
    depth_rows, x_rows, y_rows = density.shape
    rim = padded_2(density, (("gx", 1), ("gz", 0)), 1)
    rim = jnp.pad(rim, ((0, 0), (0, 0), (1, 1))).astype(jnp.float32)
    scale, growth, coupled = coupling_forward(
        rim, magnetic_f, coupling_kernel, (depth_rows, x_rows, y_rows)
    )
    weight_g, weight_m = depth_weights(lax.axis_index("gz") * depth_rows, depth_rows)
    part_g = jnp.einsum("z,zxy->xy", weight_g, density.astype(jnp.float32))
    part_m = jnp.einsum("z,zxy->xy", weight_m, coupled)
    predicted = lax.psum(jnp.stack([part_g, part_m]), "gz")
    misfit = predicted - observed
    back_g = weight_g[:, None, None] * misfit[0][None]
    back_m = weight_m[:, None, None] * misfit[1][None]
    back_scale = (back_m * magnetic_f * growth * (1.0 - scale * scale)).astype(jnp.bfloat16)
    back_shift = back_m.astype(jnp.bfloat16)
    cotangents = jnp.stack([back_scale, back_shift])
    outer = padded_2(cotangents, (("gx", 2), ("gz", 1)), 1)
    outer = jnp.pad(outer, ((0, 0), (0, 0), (0, 0), (1, 1))).astype(jnp.float32)
    spread_back = stencil_sum(outer[0], coupling_kernel[0], depth_rows, x_rows, y_rows, True)
    spread_back = spread_back + stencil_sum(
        outer[1], coupling_kernel[1], depth_rows, x_rows, y_rows, True
    )
    adjoint = jnp.stack([back_g + spread_back, back_m * growth]).astype(jnp.bfloat16)
    fourth = depth_lines(across_lines(adjoint, across_adjoint), depth_adjoint)
    gradient = whitened + jnp.einsum(
        "fzxk,ky->fzxy", fourth, factor_y, preferred_element_type=jnp.float32
    )
    return (gradient, misfit)


def solution(mesh):
    in_specs = (
        P(None, "gz", "gx", None),
        P(None, "gx", None),
        P("gx", None),
        P("gx", None),
        P(),
        P(),
    )
    out_specs = (P(None, "gz", "gx", None), P(None, "gx", None))
    return jax.shard_map(local, mesh=mesh, in_specs=in_specs, out_specs=out_specs, check_vma=False)
```

profile of v0, /device:TPU:0, one launch (start us, length us, event | category | flops | bytes accessed | tf_op | source)
XLA Modules:
  0.0 1367.9 jit_solution(581240853023325873)
XLA Ops:
  7.2 33.2 %all_gather.6 = bf16[512,512]{1,0:T(8,128)(2,1)S(1)} all-gather(bf16[64,512]{1,0:T(8,128)(2,1)} %param.9), channel_id=1, replica_groups=mesh['gx'=8,'gz'=4] {'gx'}, dimensions={0}, use_global_device_ids=true | all-gather | bytes 589824 | tf_op jit(solution)/shard_map/all_gather | solution.py:72
  56.9 53.9 %all_to_all.141 = bf16[2,16,128,512]{2,1,0,3:T(8,128)(2,1)} all-to-all(bf16[2,16,128,512]{2,1,0,3:T(8,128)(2,1)} %copy.51), channel_id=1, replica_groups=mesh['gx'=8,'gz'=4] {'gz'}, dimensions={3} | all-to-all | bytes 8388608 | tf_op jit(solution)/shard_map/all_to_all | solution.py:24
  125.8 51.6 %all_to_all.142 = bf16[2,64,128,128]{3,2,0,1:T(8,128)(2,1)} all-to-all(bf16[2,64,128,128]{3,2,0,1:T(8,128)(2,1)S(1)} %copy.53), channel_id=1, replica_groups=mesh['gx'=8,'gz'=4] {'gz'}, dimensions={1} | all-to-all | bytes 8388608 | tf_op jit(solution)/shard_map/all_to_all | solution.py:25
  191.7 117.5 %all-to-all-done.2 = bf16[2,16,128,512]{2,1,0,3:T(8,128)(2,1)} async-done(((bf16[2,16,128,512]{2,1,0,3:T(8,128)(2,1)}), bf16[2,16,128,512]{2,1,0,3:T(8,128)(2,1)}, u32[]{:S(2)}, u32[]{:S(2)}) %all-to-all-start.2) | async-done | bytes 4194336 | tf_op jit(solution)/shard_map/all_to_all | solution.py:29
  323.4 9.5 convert_bitcast_fusion.2
  332.8 12.9 copy.59
  345.7 10.5 reshape.38
  363.3 90.1 %all-to-all-done.3 = bf16[8,2,131072]{2,1,0:T(2,128)(2,1)} async-done(((bf16[8,2,131072]{2,1,0:T(2,128)(2,1)}), bf16[8,2,131072]{2,1,0:T(2,128)(2,1)}, u32[]{:S(2)}, u32[]{:S(2)}) %all-to-all-start.3) | async-done | bytes 4194336 | tf_op jit(solution)/shard_map/all_to_all | solution.py:30
  453.4 10.3 reshape.39
  463.7 9.3 copy.97
  506.6 11.2 fusion.10
  517.8 122.0 %add_add_fusion = (bf16[16,128,512]{1,2,0:T(8,128)(2,1)S(1)}, f32[16,128,512]{1,2,0:T(8,128)}) fusion(f32[16,128,512]{1,2,0:T(8,128)} %bitcast.166, f32[18,130,514]{1,2,0:T(8,128)} %fusion.10, f32[]{:T(128)} %bitcast.79, f32[]{:T(128)} %bitcast.78, f32[]{:T(128)} %bitcast.77, f32[]{:T(128)} %bitcast.76, f32[]{:T(128)} %bitcast.75, f32[]{:T(128)} %bitcast.74, ...), kind=kLoop, calls=%fused_computation.148 | loop fusion | flops 114294784 | bytes 123732184 | tf_op jit(solution)/shard_map/add | solution.py:66
  645.7 35.0 %all-reduce.4.cloned.1.call-done = f32[2,128,512]{2,1,0:T(8,128)} async-done(((f32[2,128,512]{2,1,0:T(8,128)}), f32[2,128,512]{2,1,0:T(8,128)}) %all-reduce.4.cloned.1.call-update) | async-done | bytes 524304 | tf_op jit(solution)/shard_map/psum | solution.py:111
  723.4 22.6 %fusion.1 = f32[2,18,130,514]{2,3,1,0:T(8,128)S(1)} fusion(bf16[2,1,130,512]{2,3,1,0:T(8,128)(2,1)} %collective-permute-done.7, bf16[2,1,130,512]{2,3,1,0:T(8,128)(2,1)S(1)} %collective-permute-done.6, bf16[2,16,1,512]{2,3,1,0:T(8,128)(2,1)} %copy.73, bf16[2,16,1,512]{2,3,1,0:T(8,128)(2,1)} %copy.72, bf16[1,16,128,512]{2,3,1,0:T(8,128)(2,1)S(1)} %multiply_convert_fusion, ...), kind=kLoop, calls=%fused_computation.8 | loop fusion | flops 50515920 | bytes 14414400 | tf_op jit(solution)/shard_map/convert_element_type | solution.py:119
  752.9 196.9 %fusion.84 = bf16[1,16,128,512]{2,3,1,0:T(8,128)(2,1)S(1)} fusion(f32[18,130,514]{1,2,0:T(8,128)} %get-tuple-element.5, f32[]{:T(128)} %bitcast.79, f32[]{:T(128)} %bitcast.78, f32[]{:T(128)} %bitcast.77, f32[]{:T(128)} %bitcast.76, f32[]{:T(128)} %bitcast.75, f32[]{:T(128)} %bitcast.74, f32[]{:T(128)} %bitcast.73, f32[]{:T(128)} %bitcast.72, f32[]{:T(128)} %bitcast.71, ...), kind=kLoop, calls=%fused_computation.161 | loop fusion | flops 115343360 | bytes 228852000 | tf_op jit(solution)/shard_map/stack | solution.py:124
  952.9 97.5 %all_to_all.143 = bf16[2,16,128,512]{2,1,0,3:T(8,128)(2,1)S(1)} all-to-all(bf16[2,16,128,512]{2,1,0,3:T(8,128)(2,1)S(1)} %copy.74), channel_id=1, replica_groups=mesh['gx'=8,'gz'=4] {'gx'}, dimensions={3} | all-to-all | bytes 8388608 | tf_op jit(solution)/shard_map/all_to_all | solution.py:29
  1071.0 12.9 copy.77
  1083.9 10.5 reshape.40
  1094.3 97.9 %all_to_all.144 = bf16[8,2,131072]{2,1,0:T(2,128)(2,1)} all-to-all(bf16[8,2,131072]{2,1,0:T(2,128)(2,1)} %reshape.40), channel_id=1, replica_groups=mesh['gx'=8,'gz'=4] {'gx'}, dimensions={0} | all-to-all | bytes 8388608 | tf_op jit(solution)/shard_map/all_to_all | solution.py:30
  1192.2 10.3 reshape.41
  1202.5 14.8 %copy.101 = bf16[2,16,128,8,64]{2,1,0,4,3:T(8,128)(2,1)} copy(bf16[2,16,128,8,64]{4,1,0,2,3:T(8,128)(2,1)} %bitcast.171) | data formatting | bytes 8388608 | tf_op jit(solution)/shard_map/all_to_all | solution.py:30
  1217.2 54.1 %all_to_all.145 = bf16[2,16,128,512]{2,1,0,3:T(8,128)(2,1)} all-to-all(bf16[2,16,128,512]{2,1,0,3:T(8,128)(2,1)} %bitcast.173), channel_id=1, replica_groups=mesh['gx'=8,'gz'=4] {'gz'}, dimensions={3} | all-to-all | bytes 8388608 | tf_op jit(solution)/shard_map/all_to_all | solution.py:24
  1286.5 50.7 %all_to_all.146 = bf16[2,64,128,128]{3,2,0,1:T(8,128)(2,1)S(1)} all-to-all(bf16[2,64,128,128]{3,2,0,1:T(8,128)(2,1)S(1)} %copy.84), channel_id=1, replica_groups=mesh['gx'=8,'gz'=4] {'gz'}, dimensions={1} | all-to-all | bytes 8388608 | tf_op jit(solution)/shard_map/all_to_all | solution.py:25
  1350.4 10.4 convolution_add_fusion
  (103 shorter events, 207.8 us)
Async XLA Ops:
  7.2 112.5 %copy-start = (bf16[64,64]{1,0:T(8,128)(2,1)S(1)}, bf16[64,64]{1,0:T(8,128)(2,1)}, u32[]{:S(2)}) copy-start(bf16[64,64]{1,0:T(8,128)(2,1)} %param.10) | copy-start | bytes 24580
  40.4 0.8 copy-start.7
  185.3 123.9 %all-to-all-start.2 = ((bf16[2,16,128,512]{2,1,0,3:T(8,128)(2,1)}), bf16[2,16,128,512]{2,1,0,3:T(8,128)(2,1)}, u32[]{:S(2)}, u32[]{:S(2)}) async-start(bf16[2,16,128,512]{2,1,0,3:T(8,128)(2,1)} %bitcast.174), calls=%async_computation.2 | async-start | bytes 8388608 | tf_op jit(solution)/shard_map/all_to_all | solution.py:29
  191.0 132.4 %all-gather.2.cloned.1.call-start = ((), (), s32[]{:S(2)}) async-start(), calls=%async_computation.8 | async-start | bytes 2359296 | tf_op jit(solution)/shard_map/all_gather | solution.py:71
  356.2 4.9 copy-start.11
  356.2 97.2 %all-to-all-start.3 = ((bf16[8,2,131072]{2,1,0:T(2,128)(2,1)}), bf16[8,2,131072]{2,1,0:T(2,128)(2,1)}, u32[]{:S(2)}, u32[]{:S(2)}) async-start(bf16[8,2,131072]{2,1,0:T(2,128)(2,1)} %reshape.38), calls=%async_computation.3 | async-start | bytes 8388608 | tf_op jit(solution)/shard_map/all_to_all | solution.py:30
  360.9 319.8 %all-reduce.4.cloned.1.call-start = ((), (), s32[]{:S(2)}) async-start(), calls=%async_computation.9 | async-start | bytes 1048576 | tf_op jit(solution)/shard_map/psum | solution.py:111
  485.1 11.4 collective-permute-start.1
  486.4 8.3 collective-permute-start
  498.3 4.3 copy-start.5
  498.3 4.8 copy-start.4
  499.9 6.0 collective-permute-start.2
  501.4 4.6 collective-permute-start.3
  503.1 2.8 copy-start.2
  503.2 3.4 copy-start.3
  639.8 41.0 %copy-start.10 = (f32[2,128,512]{2,1,0:T(8,128)S(1)}, f32[2,128,512]{2,1,0:T(8,128)}, u32[]{:S(2)}) copy-start(f32[2,128,512]{2,1,0:T(8,128)} %param.7) | copy-start | bytes 1572868
  689.7 4.5 copy-start.1
  697.9 8.7 collective-permute-start.4
  705.3 5.8 collective-permute-start.5
  717.2 3.0 collective-permute-start.6
  718.5 4.9 collective-permute-start.7
  752.9 196.9 %copy-start.6 = (bf16[1,16,128,512]{2,3,1,0:T(8,128)(2,1)S(1)}, bf16[1,16,128,512]{2,3,1,0:T(8,128)(2,1)}, u32[]{:S(2)}) copy-start(bf16[1,16,128,512]{2,3,1,0:T(8,128)(2,1)} %get-tuple-element.11) | copy-start | bytes 6291460
  1055.1 7.4 copy-start.12
  1343.1 7.3 copy-start.8
  (1 other events, 0.8 us)
Sparse Core Ops, SparseCore 0:
  193.9 102.6 all-gather.1
  645.8 34.8 all-reduce.3
where the time goes:
time: 1380 us; the launch traced here: 1370 us
  blocking collectives  439 us (32%)
  other arithmetic  376 us (27%)
  waiting for transfers between devices  248 us (18%)
  local copies, waits for them, and re-layouts  219 us (16%)
  matrix products  45.4 us (3%)
  starting transfers between devices  26.9 us (2%)
  between operations  14.6 us (1%)
    another operation x2, other arithmetic, local(): jnp.stack([back_g + spread_back, back_m * growth]).astype(jnp.bfloat16)  197 us
    add x1, other arithmetic, coupling_forward(): return (scale, growth, magnetic_f * growth + pre_shift)  122 us
    all_to_all x1, waiting for transfers between devices, across_lines(): lax.all_to_all(values, 'gx', split_axis=3, concat_axis=2, tiled=True)  117 us
    all_to_all x2, blocking collectives, depth_lines(): lax.all_to_all(values, 'gz', split_axis=3, concat_axis=1, tiled=True)  108 us
    all_to_all x2, blocking collectives, depth_lines(): lax.all_to_all(local_step(turned), 'gz', split_axis=1, concat_axis=3, til...  102 us
    all_to_all x1, blocking collectives, across_lines(): lax.all_to_all(local_step(turned), 'gx', split_axis=2, concat_axis=3, til...  97.9 us
    all_to_all x1, blocking collectives, across_lines(): lax.all_to_all(values, 'gx', split_axis=3, concat_axis=2, tiled=True)  97.5 us
    all_to_all x1, waiting for transfers between devices, across_lines(): lax.all_to_all(local_step(turned), 'gx', split_axis=2, concat_axis=3, til...  90.1 us
  transfers between devices with their start and end apart: 12, of which 6 were waited for; matrix products, arithmetic and copies ran while one was open for 2% of the time, Pallas kernels for 0%

commit v1 on v0

--- a/solution.py
+++ b/solution.py
@@ -5,6 +5,24 @@
 from jax.sharding import PartitionSpec as P
 
 NZ = 64
+
+
+def gather_around(shard, axis, dim):
+    ways, here, step = (lax.axis_size(axis), lax.axis_index(axis), shard.shape[dim])
+    shape = [n * ways if d == dim else n for d, n in enumerate(shard.shape)]
+    full = lax.dynamic_update_slice_in_dim(
+        jnp.zeros(shape, shard.dtype), shard, here * step, axis=dim
+    )
+    going_up = going_down = shard
+    for far in range(1, ways // 2 + 1):
+        going_up = lax.ppermute(going_up, axis, [(d, (d + 1) % ways) for d in range(ways)])
+        full = lax.dynamic_update_slice_in_dim(full, going_up, (here - far) % ways * step, axis=dim)
+        if 2 * far < ways:
+            going_down = lax.ppermute(going_down, axis, [(d, (d - 1) % ways) for d in range(ways)])
+            full = lax.dynamic_update_slice_in_dim(
+                full, going_down, (here + far) % ways * step, axis=dim
+            )
+    return full
 
 
 def padded_2(x, sides, width):
@@ -69,7 +87,7 @@
 def local(whitened, observed, lower_x, lower_y, lower_z, coupling_kernel):
     factor_x, factor_y = (
         lax.all_gather(lower_x, "gx", axis=0, tiled=True),
-        lax.all_gather(lower_y, "gx", axis=0, tiled=True),
+        gather_around(lower_y, "gx", 0),
     )
 
     def apply_depth(values):

time: 1380 us -> 1370 us (level)
  blocking collectives: 439 us -> 403 us
  waiting for transfers between devices: 248 us -> 265 us
  starting transfers between devices: 26.9 us -> 41.9 us
    all_gather x1 -> x0, blocking collectives: 33.2 us -> none  [local(): lax.all_gather(lower_y, 'gx', axis=0, tiled=True)]
    ppermute x0 -> x7, waiting for transfers between devices: none -> 17 us  [the longest x4 13.9 us: gather_around(): lax.ppermute(going_up, axis, [(d, (d + 1) % ways) for d in range(ways)])]
    ppermute x0 -> x7, starting transfers between devices: none -> 16.1 us  [the longest x3 16.1 us: gather_around(): lax.ppermute(going_down, axis, [(d, (d - 1) % ways) for d in range(ways)])]
  transfers between devices with their start and end apart: 12 -> 19, of which waited for: 6 -> 11; matrix products, arithmetic and copies ran while one was open for 2% -> 2% of each run, Pallas kernels for 0% -> 0%
where the time goes in v1:
time: 1370 us; the launch traced here: 1360 us
  blocking collectives  403 us (29%)
  other arithmetic  375 us (27%)
  waiting for transfers between devices  265 us (19%)
  local copies, waits for them, and re-layouts  214 us (16%)
  matrix products  43.8 us (3%)
  starting transfers between devices  41.9 us (3%)
  between operations  14.7 us (1%)
    another operation x2, other arithmetic, local(): jnp.stack([back_g + spread_back, back_m * growth]).astype(jnp.bfloat16)  197 us
    add x1, other arithmetic, coupling_forward(): return (scale, growth, magnetic_f * growth + pre_shift)  122 us
    all_to_all x1, waiting for transfers between devices, across_lines(): lax.all_to_all(values, 'gx', split_axis=3, concat_axis=2, tiled=True)  118 us
    all_to_all x2, blocking collectives, depth_lines(): lax.all_to_all(values, 'gz', split_axis=3, concat_axis=1, tiled=True)  106 us
    all_to_all x2, blocking collectives, depth_lines(): lax.all_to_all(local_step(turned), 'gz', split_axis=1, concat_axis=3, til...  102 us
    all_to_all x1, blocking collectives, across_lines(): lax.all_to_all(local_step(turned), 'gx', split_axis=2, concat_axis=3, til...  97.9 us
    all_to_all x1, blocking collectives, across_lines(): lax.all_to_all(values, 'gx', split_axis=3, concat_axis=2, tiled=True)  97.5 us
    all_to_all x1, waiting for transfers between devices, across_lines(): lax.all_to_all(local_step(turned), 'gx', split_axis=2, concat_axis=3, til...  90.1 us
  transfers between devices with their start and end apart: 19, of which 11 were waited for; matrix products, arithmetic and copies ran while one was open for 2% of the time, Pallas kernels for 0%

profile of v1, /device:TPU:0, one launch (start us, length us, event | category | flops | bytes accessed | tf_op | source)
XLA Modules:
  0.0 1357.9 jit_solution(6025576722862472405)
XLA Ops:
  50.3 51.6 %all_to_all.141 = bf16[2,16,128,512]{2,1,0,3:T(8,128)(2,1)} all-to-all(bf16[2,16,128,512]{2,1,0,3:T(8,128)(2,1)S(1)} %copy.51), channel_id=1, replica_groups=mesh['gx'=8,'gz'=4] {'gz'}, dimensions={3} | all-to-all | bytes 8388608 | tf_op jit(solution)/shard_map/all_to_all | solution.py:42
  101.9 9.0 copy.52
  117.0 51.6 %all_to_all.142 = bf16[2,64,128,128]{3,2,0,1:T(8,128)(2,1)} all-to-all(bf16[2,64,128,128]{3,2,0,1:T(8,128)(2,1)S(1)} %copy.53), channel_id=1, replica_groups=mesh['gx'=8,'gz'=4] {'gz'}, dimensions={1} | all-to-all | bytes 8388608 | tf_op jit(solution)/shard_map/all_to_all | solution.py:43
  181.7 117.6 %all-to-all-done.2 = bf16[2,16,128,512]{2,1,0,3:T(8,128)(2,1)} async-done(((bf16[2,16,128,512]{2,1,0,3:T(8,128)(2,1)}), bf16[2,16,128,512]{2,1,0,3:T(8,128)(2,1)}, u32[]{:S(2)}, u32[]{:S(2)}) %all-to-all-start.2) | async-done | bytes 4194336 | tf_op jit(solution)/shard_map/all_to_all | solution.py:47
  313.5 9.4 convert_bitcast_fusion.2
  323.0 12.9 copy.59
  335.9 10.5 reshape.38
  353.5 90.1 %all-to-all-done.3 = bf16[8,2,131072]{2,1,0:T(2,128)(2,1)} async-done(((bf16[8,2,131072]{2,1,0:T(2,128)(2,1)}), bf16[8,2,131072]{2,1,0:T(2,128)(2,1)}, u32[]{:S(2)}, u32[]{:S(2)}) %all-to-all-start.3) | async-done | bytes 4194336 | tf_op jit(solution)/shard_map/all_to_all | solution.py:48
  443.6 10.3 reshape.39
  453.9 9.3 copy.97
  496.7 11.2 fusion.10
  507.9 121.9 %add_add_fusion = (bf16[16,128,512]{1,2,0:T(8,128)(2,1)S(1)}, f32[16,128,512]{1,2,0:T(8,128)}) fusion(f32[16,128,512]{1,2,0:T(8,128)} %bitcast.168, f32[18,130,514]{1,2,0:T(8,128)} %fusion.10, f32[]{:T(128)} %bitcast.80, f32[]{:T(128)} %bitcast.79, f32[]{:T(128)} %bitcast.78, f32[]{:T(128)} %bitcast.77, f32[]{:T(128)} %bitcast.76, f32[]{:T(128)} %bitcast.75, ...), kind=kLoop, calls=%fused_computation.148 | loop fusion | flops 114294784 | bytes 123732184 | tf_op jit(solution)/shard_map/add | solution.py:84
  635.8 35.3 %all-reduce.4.cloned.1.call-done = f32[2,128,512]{2,1,0:T(8,128)} async-done(((f32[2,128,512]{2,1,0:T(8,128)}), f32[2,128,512]{2,1,0:T(8,128)}) %all-reduce.4.cloned.1.call-update) | async-done | bytes 524304 | tf_op jit(solution)/shard_map/psum | solution.py:129
  713.7 22.6 %fusion.1 = f32[2,18,130,514]{2,3,1,0:T(8,128)S(1)} fusion(bf16[2,1,130,512]{2,3,1,0:T(8,128)(2,1)} %collective-permute-done.14, bf16[2,1,130,512]{2,3,1,0:T(8,128)(2,1)S(1)} %collective-permute-done.13, bf16[2,16,1,512]{2,3,1,0:T(8,128)(2,1)} %copy.73, bf16[2,16,1,512]{2,3,1,0:T(8,128)(2,1)} %copy.72, bf16[1,16,128,512]{2,3,1,0:T(8,128)(2,1)S(1)} %multiply_convert_fusion, ...), kind=kLoop, calls=%fused_computation.8 | loop fusion | flops 50515920 | bytes 14414400 | tf_op jit(solution)/shard_map/convert_element_type | solution.py:137
  743.3 196.6 %fusion.83 = bf16[1,16,128,512]{2,3,1,0:T(8,128)(2,1)S(1)} fusion(f32[18,130,514]{1,2,0:T(8,128)} %get-tuple-element.5, f32[]{:T(128)} %bitcast.80, f32[]{:T(128)} %bitcast.79, f32[]{:T(128)} %bitcast.78, f32[]{:T(128)} %bitcast.77, f32[]{:T(128)} %bitcast.76, f32[]{:T(128)} %bitcast.75, f32[]{:T(128)} %bitcast.74, f32[]{:T(128)} %bitcast.73, f32[]{:T(128)} %bitcast.72, ...), kind=kLoop, calls=%fused_computation.161 | loop fusion | flops 115343360 | bytes 228852000 | tf_op jit(solution)/shard_map/stack | solution.py:142
  943.0 97.5 %all_to_all.143 = bf16[2,16,128,512]{2,1,0,3:T(8,128)(2,1)S(1)} all-to-all(bf16[2,16,128,512]{2,1,0,3:T(8,128)(2,1)S(1)} %copy.74), channel_id=1, replica_groups=mesh['gx'=8,'gz'=4] {'gx'}, dimensions={3} | all-to-all | bytes 8388608 | tf_op jit(solution)/shard_map/all_to_all | solution.py:47
  1061.0 12.9 copy.77
  1073.9 10.5 reshape.40
  1084.4 97.9 %all_to_all.144 = bf16[8,2,131072]{2,1,0:T(2,128)(2,1)} all-to-all(bf16[8,2,131072]{2,1,0:T(2,128)(2,1)} %reshape.40), channel_id=1, replica_groups=mesh['gx'=8,'gz'=4] {'gx'}, dimensions={0} | all-to-all | bytes 8388608 | tf_op jit(solution)/shard_map/all_to_all | solution.py:48
  1182.2 10.3 reshape.41
  1192.5 14.8 %copy.101 = bf16[2,16,128,8,64]{2,1,0,4,3:T(8,128)(2,1)} copy(bf16[2,16,128,8,64]{4,1,0,2,3:T(8,128)(2,1)} %bitcast.173) | data formatting | bytes 8388608 | tf_op jit(solution)/shard_map/all_to_all | solution.py:48
  1207.3 54.1 %all_to_all.145 = bf16[2,16,128,512]{2,1,0,3:T(8,128)(2,1)} all-to-all(bf16[2,16,128,512]{2,1,0,3:T(8,128)(2,1)} %bitcast.175), channel_id=1, replica_groups=mesh['gx'=8,'gz'=4] {'gz'}, dimensions={3} | all-to-all | bytes 8388608 | tf_op jit(solution)/shard_map/all_to_all | solution.py:42
  1276.5 50.7 %all_to_all.146 = bf16[2,64,128,128]{3,2,0,1:T(8,128)(2,1)S(1)} all-to-all(bf16[2,64,128,128]{3,2,0,1:T(8,128)(2,1)S(1)} %copy.84), channel_id=1, replica_groups=mesh['gx'=8,'gz'=4] {'gz'}, dimensions={1} | all-to-all | bytes 8388608 | tf_op jit(solution)/shard_map/all_to_all | solution.py:43
  1340.4 10.4 convolution_add_fusion
  (125 shorter events, 224.2 us)
Async XLA Ops:
  7.2 103.7 %copy-start = (bf16[64,64]{1,0:T(8,128)(2,1)S(1)}, bf16[64,64]{1,0:T(8,128)(2,1)}, u32[]{:S(2)}) copy-start(bf16[64,64]{1,0:T(8,128)(2,1)} %param.10) | copy-start | bytes 24580
  7.2 8.3 collective-permute-start.1
  13.2 7.2 collective-permute-start
  15.5 6.9 collective-permute-start.3
  20.4 7.0 collective-permute-start.2
  22.3 12.1 collective-permute-start.5
  27.4 7.0 collective-permute-start.4
  34.4 7.0 collective-permute-start.6
  176.4 122.9 %all-to-all-start.2 = ((bf16[2,16,128,512]{2,1,0,3:T(8,128)(2,1)}), bf16[2,16,128,512]{2,1,0,3:T(8,128)(2,1)}, u32[]{:S(2)}, u32[]{:S(2)}) async-start(bf16[2,16,128,512]{2,1,0,3:T(8,128)(2,1)} %bitcast.176), calls=%async_computation.2 | async-start | bytes 8388608 | tf_op jit(solution)/shard_map/all_to_all | solution.py:47
  181.0 132.6 %all-gather.2.cloned.1.call-start = ((), (), s32[]{:S(2)}) async-start(), calls=%async_computation.8 | async-start | bytes 2359296 | tf_op jit(solution)/shard_map/all_gather | solution.py:89
  346.4 97.2 %all-to-all-start.3 = ((bf16[8,2,131072]{2,1,0:T(2,128)(2,1)}), bf16[8,2,131072]{2,1,0:T(2,128)(2,1)}, u32[]{:S(2)}, u32[]{:S(2)}) async-start(bf16[8,2,131072]{2,1,0:T(2,128)(2,1)} %reshape.38), calls=%async_computation.3 | async-start | bytes 8388608 | tf_op jit(solution)/shard_map/all_to_all | solution.py:48
  351.1 320.0 %all-reduce.4.cloned.1.call-start = ((), (), s32[]{:S(2)}) async-start(), calls=%async_computation.9 | async-start | bytes 1048576 | tf_op jit(solution)/shard_map/psum | solution.py:129
  475.3 11.4 collective-permute-start.8
  476.6 8.3 collective-permute-start.7
  490.1 6.0 collective-permute-start.9
  491.5 4.7 collective-permute-start.10
  629.9 41.2 %copy-start.10 = (f32[2,128,512]{2,1,0:T(8,128)S(1)}, f32[2,128,512]{2,1,0:T(8,128)}, u32[]{:S(2)}) copy-start(f32[2,128,512]{2,1,0:T(8,128)} %param.7) | copy-start | bytes 1572868
  688.2 8.7 collective-permute-start.11
  695.6 5.8 collective-permute-start.12
  707.5 3.0 collective-permute-start.13
  708.9 4.9 collective-permute-start.14
  743.3 196.6 %copy-start.6 = (bf16[1,16,128,512]{2,3,1,0:T(8,128)(2,1)S(1)}, bf16[1,16,128,512]{2,3,1,0:T(8,128)(2,1)}, u32[]{:S(2)}) copy-start(bf16[1,16,128,512]{2,3,1,0:T(8,128)(2,1)} %get-tuple-element.11) | copy-start | bytes 6291460
  1045.1 7.5 copy-start.12
  1333.2 7.3 copy-start.8
  (8 other events, 31.8 us)
Sparse Core Ops, SparseCore 0:
  183.9 102.8 all-gather.1
  635.9 35.1 all-reduce.3
